TPU v7x, 128 devices: a whole 4x4x4 slice. The times are simulated.
128 devices in a mesh: sec: 32 (over y, x_hi, z), tile: 4 (over x_lo, core).
Axes of the slice: x: 4 (x_hi: 2, x_lo: 2; x = x_hi * 2 + x_lo), y: 4, z: 4, core: 2. Of those that a mesh axis runs over, the one named last changes fastest.
Arguments:
- images: bfloat16 [64, 128, 256], P('sec', 'tile'), may hold values from -6 to 6
- seam_links: int32 [64, 3], replicated, may hold values 0 or 1
- partners: int32 [64, 3], P('sec'), may hold values from 0 to 63, as said below
- enc_first: bfloat16 [64, 1, 3, 3], replicated, may hold values from -3 to 3
- enc_second: bfloat16 [64, 64, 3, 3], replicated, may hold values from -0.375 to 0.375
- enc_third: bfloat16 [32, 64, 1, 1], replicated, may hold values from -1 to 1
- dec_first: bfloat16 [64, 81, 3, 3], replicated, may hold values from -0.3125 to 0.3125
- dec_second: bfloat16 [64, 64, 3, 3], replicated, may hold values from -0.375 to 0.375
- dec_third: bfloat16 [2, 64, 3, 3], replicated, may hold values from -0.375 to 0.375
Outputs:
- descriptors: bfloat16 [64, 32, 64, 128], P('sec', None, 'tile')
- flows: float32 [64, 3, 2, 64, 128], P('sec', None, None, 'tile')
Inputs may be any that keep to these rules, and one draw needn't show every extreme that they name: partners[s, j] is s + o or s - o, with o = 1, 2, 4 for j = 0, 1, 2.
All inputs are finite; a program needn't handle non-finite values.
Results may differ from a plain program's by a relative error of at most 0.0098.
Values may be sent and summed in bfloat16 or wider, within the bound.
A program may use at most 128 MiB of HBM per device.

v0:
```python
import functools
import math

import jax
import jax.numpy as jnp
from jax import lax
from jax.experimental import pallas as pl
from jax.experimental.pallas import tpu as pltpu
from jax.sharding import PartitionSpec as P

MESH = pl.DeviceIdType.MESH
F32, BF16 = jnp.float32, jnp.bfloat16

RADIUS = 4
SPAN = 2 * RADIUS + 1
DISP = SPAN * SPAN
OFFSETS = (1, 2, 4)
ROWS = 16
COLS = 128
CH = 64
DESC = 32
K1 = 248
EXT = ROWS + 2 * RADIUS


def leaky(v):
    return jnp.maximum(v, 0.1 * v)


def dot(a, b):
    return jnp.dot(a, b, preferred_element_type=F32)


def fold(out, half, shift, rows):
    lane = lax.broadcasted_iota(jnp.int32, (rows, COLS), 1)
    cols = slice(half * COLS, (half + 1) * COLS)
    left = pltpu.roll(out[0:rows, cols], shift, 1)
    right = pltpu.roll(out[2 * rows : 3 * rows, cols], COLS - shift, 1)
    return (
        jnp.where(lane >= shift, left, 0.0)
        + out[rows : 2 * rows, cols]
        + jnp.where(lane < COLS - shift, right, 0.0)
    )


def kernel(
    n_sec, n_tile, seam, partners, img, w1, w2, w3, d1, d2, d3, desc_out, flow_out,
    img_lo, img_hi, taps, pick, w1m, w2m, w3m, d1m, d2m, d3m, first3, desc_cy, own_rot, held, part,
    cost3, edge_out, edge_in, hid1, hid2, flow_y,
    img_send, img_recv, sec_send, sec_recv, rim_send, rim_recv, edge_send, edge_recv,
):
    sec, tile = lax.axis_index("sec"), lax.axis_index("tile")

    def at(k, dt):
        return (lax.rem(sec + k + n_sec, n_sec), lax.rem(tile + dt + n_tile, n_tile))

    peers = [(k, dt) for k in (0, -1, 1, -2, 2) for dt in (-1, 0, 1) if (k, dt) != (0, 0)]
    barrier = pltpu.get_barrier_semaphore()
    for k, dt in peers:
        pl.semaphore_signal(barrier, inc=1, device_id=at(k, dt), device_id_type=MESH)

    row_i = lax.broadcasted_iota(jnp.int32, (2 * COLS, COLS), 0)
    col_i = lax.broadcasted_iota(jnp.int32, (2 * COLS, COLS), 1)
    for kx in range(3):
        pick[:, kx * COLS : (kx + 1) * COLS] = jnp.where(row_i == 2 * col_i + (kx - 1), 1.0, 0.0).astype(BF16)
    taps[...] = jnp.zeros_like(taps)
    w1f = w1[...].astype(F32)
    for ky in range(3):
        taps[3 * ky : 3 * ky + 3, 0:CH] = w1f[ky]
    w1m[...] = taps[0:COLS, :].T[0:CH, 0:16].astype(BF16)
    w3m[...] = w3[...]
    for kx in range(3):
        rows = slice(kx * CH, (kx + 1) * CH)
        w2m[rows, :] = jnp.concatenate([w2[ky, kx].astype(F32) for ky in range(3)], axis=1).astype(BF16)
        d2m[rows, :] = jnp.concatenate([d2[ky, kx].astype(F32) for ky in range(3)], axis=1).astype(BF16)
        d1m[rows, :] = jnp.concatenate(
            [d1[ky, kx].astype(F32) for ky in range(3)] + [jnp.zeros((CH, K1 - 3 * DISP), F32)], axis=1
        ).astype(BF16)
    d3m[...] = jnp.zeros_like(d3m)
    for kx in range(3):
        d3m[kx * 8 : kx * 8 + 2, :] = jnp.concatenate([d3[ky, kx].astype(F32) for ky in range(3)], axis=1)
    for n in range(6):
        for y in range(ROWS + 2):
            cost3[n, y * K1 + 240 : y * K1 + K1, :] = jnp.zeros((8, COLS), F32)

    def link(section, side):
        place = tile - 1 + side
        inside = jnp.logical_and(place >= 0, place < n_tile - 1)
        place = jnp.clip(place, 0, n_tile - 2)
        section = jnp.clip(section, 0, 2 * n_sec - 1)
        return jnp.where(inside, seam[place, section], 0).astype(F32)

    pl.semaphore_wait(barrier, len(peers))

    def img_copy(direction):
        if direction == 0:
            src, dst, dt = img.at[:, 16:32, :], img_lo, 1
        else:
            src, dst, dt = img.at[:, 0:16, :], img_hi, -1
        return pltpu.make_async_remote_copy(
            src_ref=src, dst_ref=dst, send_sem=img_send.at[direction], recv_sem=img_recv.at[direction],
            device_id=at(0, dt), device_id_type=MESH,
        )

    for direction in (0, 1):
        img_copy(direction).start()
    for direction in (0, 1):
        img_copy(direction).wait()

    base = 2 * sec

    def encode(s, carry):
        lower, upper = link(base + s, 0), link(base + s, 1)
        below = dot(img_lo[s], pick[...]) * lower
        mid = dot(img[s], pick[...])
        above = dot(img_hi[s], pick[...]) * upper
        for kx in range(3):
            cols = slice(kx * COLS, (kx + 1) * COLS)
            taps[pl.ds(kx, 16, stride=3), :] = below[:, cols]
            taps[pl.ds(48 + kx, 32, stride=3), :] = mid[:, cols]
            taps[pl.ds(144 + kx, 16, stride=3), :] = above[:, cols]

        def first(p, carry):
            x = jnp.concatenate([taps[pl.ds(12 * p + 33, 16), :], taps[pl.ds(12 * p + 39, 16), :]], axis=1)
            v = leaky(dot(w1m[...], x.astype(BF16))) * jnp.where(p == 9, upper, 1.0)
            v = v.astype(BF16)
            for h in range(2):
                vh = v[:, h * COLS : (h + 1) * COLS]
                first3[2 * p + h + 4, 0:CH, :] = vh
                first3[2 * p + h + 2, CH : 2 * CH, :] = vh
                first3[2 * p + h, 2 * CH : 3 * CH, :] = vh
            return carry

        lax.fori_loop(0, 10, first, 0)

        def second(q, carry):
            x = jnp.concatenate([first3[2 * q + 4], first3[2 * q + 5]], axis=1)
            o = dot(w2m[...], x)
            z = jnp.concatenate([leaky(fold(o, h, 2, CH)).astype(BF16) for h in range(2)], axis=1)
            d = dot(w3m[...], z).astype(BF16)
            for h in range(2):
                dh = d[:, h * COLS : (h + 1) * COLS]
                held[4 + s, RADIUS + 2 * q + h] = dh
                desc_cy[s, pl.ds(2 * q + h, DESC, stride=ROWS), :] = dh.astype(F32)
            return carry

        lax.fori_loop(0, ROWS // 2, second, 0)
        return carry

    lax.fori_loop(0, 2, encode, 0)

    def sec_copy(k, i):
        return pltpu.make_async_remote_copy(
            src_ref=held.at[4:6, RADIUS : RADIUS + ROWS],
            dst_ref=held.at[4 - 2 * k : 6 - 2 * k, RADIUS : RADIUS + ROWS],
            send_sem=sec_send.at[i], recv_sem=sec_recv.at[i],
            device_id=at(k, 0), device_id_type=MESH,
        )

    def rim_copy(k, dt, i):
        if dt < 0:
            src, dst = slice(RADIUS, 2 * RADIUS), slice(RADIUS + ROWS, EXT)
        else:
            src, dst = slice(ROWS, RADIUS + ROWS), slice(0, RADIUS)
        return pltpu.make_async_remote_copy(
            src_ref=held.at[4:6, src],
            dst_ref=held.at[4 - 2 * k : 6 - 2 * k, dst],
            send_sem=rim_send.at[i], recv_sem=rim_recv.at[i],
            device_id=at(k, dt), device_id_type=MESH,
        )

    near = [sec_copy(-1, 0), sec_copy(1, 1)]
    near += [rim_copy(k, dt, 2 * i + (dt > 0)) for i, k in enumerate((0, -1, 1)) for dt in (-1, 1)]
    far = [sec_copy(-2, 2), sec_copy(2, 3)]
    far += [rim_copy(k, dt, 6 + 2 * i + (dt > 0)) for i, k in enumerate((-2, 2)) for dt in (-1, 1)]
    for copy in near + far:
        copy.start()

    lane = lax.broadcasted_iota(jnp.int32, (COLS, COLS), 1)

    def spread(i, carry):
        s, chunk = i // 4, lax.rem(i, 4)
        rows = pl.ds(pl.multiple_of(chunk * COLS, COLS), COLS)
        own = desc_cy[s, rows, :]
        desc_out[s, pl.ds(chunk * 8, 8)] = own.reshape(8, ROWS, COLS).astype(BF16)
        scaled = own * (1.0 / math.sqrt(DESC))
        for b in range(SPAN):
            d = b - RADIUS
            moved = pltpu.roll(scaled, d % COLS, 1) if d else scaled
            keep = jnp.logical_and(lane - d >= 0, lane - d < COLS)
            own_rot[s, b, rows, :] = jnp.where(keep, moved, 0.0)
        return carry

    lax.fori_loop(0, 8, spread, 0)

    def edge_copy(stage, n, direction):
        if stage == 0:
            src, dst = edge_out.at[n, direction], edge_in.at[n, direction]
        else:
            buf = (hid1, hid2)[stage - 1]
            if direction == 0:
                src, dst = buf.at[n, 1, CH : 2 * CH], buf.at[n, ROWS, 2 * CH : 3 * CH]
            else:
                src, dst = buf.at[n, ROWS, CH : 2 * CH], buf.at[n, 1, 0:CH]
        return pltpu.make_async_remote_copy(
            src_ref=src, dst_ref=dst,
            send_sem=edge_send.at[stage, n, direction], recv_sem=edge_recv.at[stage, n, direction],
            device_id=at(0, 2 * direction - 1), device_id_type=MESH,
        )

    def correlate(j, s):
        n = 2 * j + s
        offset = OFFSETS[j]
        own_id = base + s
        flag = partners[s, j] == own_id + offset
        lower = jnp.where(flag, link(own_id + offset, 0), link(own_id - offset, 0))
        upper = jnp.where(flag, link(own_id + offset, 1), link(own_id - offset, 1))

        def gather(y, carry):
            ahead = held[4 + s + offset, y].astype(F32)
            behind = held[4 + s - offset, y].astype(F32)
            m = jnp.where(y < RADIUS, lower, jnp.where(y >= RADIUS + ROWS, upper, 1.0))
            part[pl.ds(y, DESC, stride=EXT), :] = jnp.where(flag, ahead, behind) * m
            return carry

        lax.fori_loop(0, EXT, gather, 0)

        def column(b, carry):
            def channel(c, acc):
                own = own_rot[s, b, pl.ds(pl.multiple_of(c * ROWS, ROWS), ROWS), :]
                start = pl.multiple_of(c * EXT, 8)
                return tuple(acc[a] + own * part[pl.ds(start + a, ROWS), :] for a in range(SPAN))

            acc = lax.fori_loop(
                0, DESC, channel, tuple(jnp.zeros((ROWS, COLS), F32) for _ in range(SPAN)), unroll=4
            )
            shift = lax.rem(COLS + RADIUS - b, COLS)
            for a in range(SPAN):
                moved = pltpu.roll(acc[a], shift, 1)
                d = a * SPAN + b
                for ky in range(3):
                    cost3[n, pl.ds((2 - ky) * K1 + ky * DISP + d, ROWS, stride=K1), :] = moved
            return carry

        lax.fori_loop(0, SPAN, column, 0)
        edge_out[n, 0] = cost3[n, K1 + DISP : K1 + DISP + 88, :]
        edge_out[n, 1] = cost3[n, ROWS * K1 + DISP : ROWS * K1 + DISP + 88, :]
        for direction in (0, 1):
            edge_copy(0, n, direction).start()

    for j in range(3):
        if j == 0:
            for copy in near:
                copy.wait_recv()
        if j == 2:
            for copy in far:
                copy.wait_recv()

        def one(s, carry, j=j):
            correlate(j, s)
            return carry

        lax.fori_loop(0, 2, one, 0)

    def hidden_rows(n, q, o, buf):
        for h in range(2):
            v = leaky(fold(o, h, 1, CH)).astype(BF16)
            for ky in range(3):
                buf[n, 2 * q + h + 2 - ky, ky * CH : (ky + 1) * CH, :] = v

    def decode_one(n, carry):
        s = lax.rem(n, 2)
        for direction in (0, 1):
            edge_copy(0, n, direction).wait_recv()
        cost3[n, K1 : K1 + DISP, :] = edge_in[n, 1, 0:DISP, :] * link(base + s, 0)
        cost3[n, ROWS * K1 + 2 * DISP : ROWS * K1 + 3 * DISP, :] = edge_in[n, 0, 0:DISP, :] * link(base + s, 1)

        def rows(q, carry):
            start = pl.multiple_of((2 * q + 1) * K1, 8)
            x = jnp.concatenate([cost3[n, pl.ds(start, K1), :], cost3[n, pl.ds(start + K1, K1), :]], axis=1)
            hidden_rows(n, q, dot(d1m[...], x.astype(BF16)), hid1)
            return carry

        lax.fori_loop(0, ROWS // 2, rows, 0)
        for direction in (0, 1):
            edge_copy(1, n, direction).start()
        return carry

    lax.fori_loop(0, 6, decode_one, 0)

    def rims(stage, n, buf):
        s = lax.rem(n, 2)
        for direction in (0, 1):
            edge_copy(stage, n, direction).wait_recv()
        buf[n, 1, 0:CH, :] = (buf[n, 1, 0:CH, :].astype(F32) * link(base + s, 0)).astype(BF16)
        top = slice(2 * CH, 3 * CH)
        buf[n, ROWS, top, :] = (buf[n, ROWS, top, :].astype(F32) * link(base + s, 1)).astype(BF16)

    def decode_two(n, carry):
        rims(1, n, hid1)

        def rows(q, carry):
            x = jnp.concatenate([hid1[n, 2 * q + 1], hid1[n, 2 * q + 2]], axis=1)
            hidden_rows(n, q, dot(d2m[...], x), hid2)
            return carry

        lax.fori_loop(0, ROWS // 2, rows, 0)
        for direction in (0, 1):
            edge_copy(2, n, direction).start()
        return carry

    lax.fori_loop(0, 6, decode_two, 0)

    def decode_three(n, carry):
        rims(2, n, hid2)
        weights = d3m[...].astype(BF16)

        def rows(q, carry):
            x = jnp.concatenate([hid2[n, 2 * q + 1], hid2[n, 2 * q + 2]], axis=1)
            o = dot(weights, x)
            for h in range(2):
                flow_y[pl.ds(pl.multiple_of((2 * q + h) * 8, 8), 8), :] = fold(o, h, 1, 8)
            return carry

        lax.fori_loop(0, ROWS // 2, rows, 0)
        s, j = lax.rem(n, 2), n // 2
        for o in range(2):
            flow_out[s, j, o] = flow_y[pl.ds(o, ROWS, stride=8), :]
        return carry

    lax.fori_loop(0, 6, decode_three, 0)

    for direction in (0, 1):
        pass
    for copy in near + far:
        copy.wait_send()

    def drain(n, carry):
        for stage in range(3):
            for direction in (0, 1):
                edge_copy(stage, n, direction).wait_send()
        return carry

    lax.fori_loop(0, 6, drain, 0)


def solution(mesh):
    n_sec, n_tile = mesh.shape["sec"], mesh.shape["tile"]
    vmem = pl.BlockSpec(memory_space=pltpu.VMEM)
    smem = pl.BlockSpec(memory_space=pltpu.SMEM)
    dma = pltpu.SemaphoreType.DMA

    def shards(images, seam_links, partners, enc_first, enc_second, enc_third, dec_first, dec_second, dec_third):
        taps_first = lambda w: jnp.transpose(w, (2, 3, 0, 1))
        return pl.pallas_call(
            functools.partial(kernel, n_sec, n_tile),
            out_shape=(
                jax.ShapeDtypeStruct((2, DESC, ROWS, COLS), BF16),
                jax.ShapeDtypeStruct((2, 3, 2, ROWS, COLS), F32),
            ),
            in_specs=[smem, smem] + [vmem] * 7,
            out_specs=(vmem, vmem),
            scratch_shapes=[
                pltpu.VMEM((2, 16, 256), BF16),
                pltpu.VMEM((2, 16, 256), BF16),
                pltpu.VMEM((192, COLS), F32),
                pltpu.VMEM((256, 3 * COLS), BF16),
                pltpu.VMEM((CH, 16), BF16),
                pltpu.VMEM((3 * CH, 3 * CH), BF16),
                pltpu.VMEM((DESC, CH), BF16),
                pltpu.VMEM((3 * CH, K1), BF16),
                pltpu.VMEM((3 * CH, 3 * CH), BF16),
                pltpu.VMEM((24, 3 * CH), F32),
                pltpu.VMEM((24, 3 * CH, COLS), BF16),
                pltpu.VMEM((2, DESC * ROWS, COLS), F32),
                pltpu.VMEM((2, SPAN, DESC * ROWS, COLS), F32),
                pltpu.VMEM((10, EXT, DESC, COLS), BF16),
                pltpu.VMEM((DESC * EXT, COLS), F32),
                pltpu.VMEM((6, (ROWS + 2) * K1, COLS), F32),
                pltpu.VMEM((6, 2, 88, COLS), F32),
                pltpu.VMEM((6, 2, 88, COLS), F32),
                pltpu.VMEM((6, ROWS + 2, 3 * CH, COLS), BF16),
                pltpu.VMEM((6, ROWS + 2, 3 * CH, COLS), BF16),
                pltpu.VMEM((ROWS * 8, COLS), F32),
                dma((2,)), dma((2,)), dma((4,)), dma((4,)), dma((10,)), dma((10,)),
                dma((3, 6, 2)), dma((3, 6, 2)),
            ],
            compiler_params=pltpu.CompilerParams(
                collective_id=0, has_side_effects=True, vmem_limit_bytes=56 * 1024 * 1024
            ),
        )(
            jnp.transpose(seam_links), partners, images,
            jnp.transpose(enc_first, (1, 2, 3, 0))[0], taps_first(enc_second), taps_first(enc_third)[0, 0],
            taps_first(dec_first), taps_first(dec_second), taps_first(dec_third),
        )

    return jax.shard_map(
        shards,
        mesh=mesh,
        in_specs=(P("sec", "tile", None), P(), P("sec", None), P(), P(), P(), P(), P(), P()),
        out_specs=(P("sec", None, "tile", None), P("sec", None, None, "tile", None)),
        check_vma=False,
    )
```

profile of v0, /device:TPU:1, one launch (start us, length us, event | category | flops | bytes accessed | tf_op | source)
XLA Modules:
  0.0 100.1 jit_solution(87026242846158231)
XLA Ops:
  0.6 97.1 %shard_map.104 = (bf16[2,32,16,128]{3,2,1,0:T(8,128)(2,1)}, f32[2,3,2,16,128]{4,3,2,1,0:T(8,128)}) custom-call(s32[3,64]{1,0:T(4,128)} %bitcast.15, s32[2,3]{1,0:T(2,128)} %partners.1, bf16[2,32,256]{2,1,0:T(8,128)(2,1)} %img.1, bf16[3,3,64]{2,1,0:T(4,128)(2,1)} %bitcast.14, bf16[3,3,64,64]{3,2,1,0:T(8,128)(2,1)} %bitcast.9, bf16[32,64]{1,0:T(8,128)(2,1)} %bitcast.12, ...), custom_call_target="tpu_custom_call" | custom-call | tf_op jit(solution)/shard_map/pallas_call | solution.py:355
  97.7 0.0 copy-start
  97.7 1.7 %copy.13 = bf16[2,32,16,128]{3,2,1,0:T(8,128)(2,1)} copy(bf16[2,32,16,128]{3,2,1,0:T(8,128)(2,1)} %get-tuple-element.4) | data formatting | bytes 524288
  99.4 0.0 copy-done
  99.4 0.6 copy.14
Async XLA Ops:
  97.7 1.7 %copy-start = (f32[2,3,2,16,128]{4,3,2,1,0:T(8,128)S(1)}, f32[2,3,2,16,128]{4,3,2,1,0:T(8,128)}, u32[]{:S(2)}) copy-start(f32[2,3,2,16,128]{4,3,2,1,0:T(8,128)} %get-tuple-element.5) | copy-start | bytes 294916
where the time goes:
time: 101 us; the launch traced here: 100 us
  Pallas kernels  97.1 us (96%)
  local copies, waits for them, and re-layouts  2.35 us (2%)
    pallas_call x1, Pallas kernels, shards(): pl.pallas_call(functools.partial(kernel, n_sec, n_tile), out_shape=(jax.S...  97.1 us
    unnamed x4, local copies, waits for them, and re-layouts  2.35 us

commit v1 on v0

--- a/solution.py
+++ b/solution.py
@@ -45,9 +45,9 @@
 
 def kernel(
     n_sec, n_tile, seam, partners, img, w1, w2, w3, d1, d2, d3, desc_out, flow_out,
-    img_lo, img_hi, taps, pick, w1m, w2m, w3m, d1m, d2m, d3m, first3, desc_cy, own_rot, held, part,
+    own_img, far_img, taps, pick, w1m, w2m, w3m, d1m, d2m, d3m, first3, desc_cy, own_rot, held, part, far_part,
     cost3, edge_out, edge_in, hid1, hid2, flow_y,
-    img_send, img_recv, sec_send, sec_recv, rim_send, rim_recv, edge_send, edge_recv,
+    img_send, img_recv, near_send, near_recv, edge_send, edge_recv,
 ):
     sec, tile = lax.axis_index("sec"), lax.axis_index("tile")
 
@@ -68,6 +68,28 @@
     for ky in range(3):
         taps[3 * ky : 3 * ky + 3, 0:CH] = w1f[ky]
     w1m[...] = taps[0:COLS, :].T[0:CH, 0:16].astype(BF16)
+
+    def link(section, side):
+        place = tile - 1 + side
+        inside = jnp.logical_and(place >= 0, place < n_tile - 1)
+        place = jnp.clip(place, 0, n_tile - 2)
+        section = jnp.clip(section, 0, 2 * n_sec - 1)
+        return jnp.where(inside, seam[place, section], 0).astype(F32)
+
+    pl.semaphore_wait(barrier, len(peers))
+
+    def img_copy(k, dt, i):
+        dst = own_img if k == 0 else far_img.at[int(k < 0)]
+        src, rows = {-1: (img.at[:, 0:16], slice(48, 64)), 0: (img, slice(16, 48)), 1: (img.at[:, 16:32], slice(0, 16))}[dt]
+        return pltpu.make_async_remote_copy(
+            src_ref=src, dst_ref=dst.at[:, rows], send_sem=img_send.at[i], recv_sem=img_recv.at[i],
+            device_id=at(k, dt), device_id_type=MESH,
+        )
+
+    img_copies = [img_copy(k, dt, i) for i, (k, dt) in enumerate([p for p in peers if p[0] in (0, -2, 2)])]
+    for copy in img_copies:
+        copy.start()
+
     w3m[...] = w3[...]
     for kx in range(3):
         rows = slice(kx * CH, (kx + 1) * CH)
@@ -83,98 +105,97 @@
         for y in range(ROWS + 2):
             cost3[n, y * K1 + 240 : y * K1 + K1, :] = jnp.zeros((8, COLS), F32)
 
-    def link(section, side):
-        place = tile - 1 + side
-        inside = jnp.logical_and(place >= 0, place < n_tile - 1)
-        place = jnp.clip(place, 0, n_tile - 2)
-        section = jnp.clip(section, 0, 2 * n_sec - 1)
-        return jnp.where(inside, seam[place, section], 0).astype(F32)
-
-    pl.semaphore_wait(barrier, len(peers))
-
-    def img_copy(direction):
-        if direction == 0:
-            src, dst, dt = img.at[:, 16:32, :], img_lo, 1
-        else:
-            src, dst, dt = img.at[:, 0:16, :], img_hi, -1
-        return pltpu.make_async_remote_copy(
-            src_ref=src, dst_ref=dst, send_sem=img_send.at[direction], recv_sem=img_recv.at[direction],
-            device_id=at(0, dt), device_id_type=MESH,
-        )
-
-    for direction in (0, 1):
-        img_copy(direction).start()
-    for direction in (0, 1):
-        img_copy(direction).wait()
+    for copy in img_copies[:2]:
+        copy.wait_recv()
 
     base = 2 * sec
 
-    def encode(s, carry):
-        lower, upper = link(base + s, 0), link(base + s, 1)
-        below = dot(img_lo[s], pick[...]) * lower
-        mid = dot(img[s], pick[...])
-        above = dot(img_hi[s], pick[...]) * upper
+    def encode(below, mid, above, lower, upper, rim, write):
+        below = dot(below, pick[...]) * lower
+        mid = dot(mid, pick[...])
+        above = dot(above, pick[...]) * upper
         for kx in range(3):
             cols = slice(kx * COLS, (kx + 1) * COLS)
             taps[pl.ds(kx, 16, stride=3), :] = below[:, cols]
             taps[pl.ds(48 + kx, 32, stride=3), :] = mid[:, cols]
             taps[pl.ds(144 + kx, 16, stride=3), :] = above[:, cols]
 
-        def first(p, carry):
-            x = jnp.concatenate([taps[pl.ds(12 * p + 33, 16), :], taps[pl.ds(12 * p + 39, 16), :]], axis=1)
-            v = leaky(dot(w1m[...], x.astype(BF16))) * jnp.where(p == 9, upper, 1.0)
+        for y in range(-rim - 2, ROWS + rim + 2, 2):
+            at_row = 6 * y + 45
+            x = jnp.concatenate([taps[at_row : at_row + 16, :], taps[at_row + 6 : at_row + 22, :]], axis=1)
+            v = leaky(dot(w1m[...], x.astype(BF16)))
+            if y >= ROWS:
+                v = v * upper
             v = v.astype(BF16)
             for h in range(2):
                 vh = v[:, h * COLS : (h + 1) * COLS]
-                first3[2 * p + h + 4, 0:CH, :] = vh
-                first3[2 * p + h + 2, CH : 2 * CH, :] = vh
-                first3[2 * p + h, 2 * CH : 3 * CH, :] = vh
-            return carry
-
-        lax.fori_loop(0, 10, first, 0)
-
-        def second(q, carry):
-            x = jnp.concatenate([first3[2 * q + 4], first3[2 * q + 5]], axis=1)
+                for ky in range(3):
+                    to = y + h + 2 - 2 * ky
+                    if -rim <= to < ROWS + rim:
+                        first3[to + RADIUS, ky * CH : (ky + 1) * CH, :] = vh
+
+        for y in range(-rim, ROWS + rim, 2):
+            x = jnp.concatenate([first3[y + RADIUS], first3[y + RADIUS + 1]], axis=1)
             o = dot(w2m[...], x)
             z = jnp.concatenate([leaky(fold(o, h, 2, CH)).astype(BF16) for h in range(2)], axis=1)
             d = dot(w3m[...], z).astype(BF16)
             for h in range(2):
-                dh = d[:, h * COLS : (h + 1) * COLS]
-                held[4 + s, RADIUS + 2 * q + h] = dh
-                desc_cy[s, pl.ds(2 * q + h, DESC, stride=ROWS), :] = dh.astype(F32)
-            return carry
-
-        lax.fori_loop(0, ROWS // 2, second, 0)
-        return carry
-
-    lax.fori_loop(0, 2, encode, 0)
-
-    def sec_copy(k, i):
-        return pltpu.make_async_remote_copy(
-            src_ref=held.at[4:6, RADIUS : RADIUS + ROWS],
-            dst_ref=held.at[4 - 2 * k : 6 - 2 * k, RADIUS : RADIUS + ROWS],
-            send_sem=sec_send.at[i], recv_sem=sec_recv.at[i],
-            device_id=at(k, 0), device_id_type=MESH,
-        )
-
-    def rim_copy(k, dt, i):
-        if dt < 0:
-            src, dst = slice(RADIUS, 2 * RADIUS), slice(RADIUS + ROWS, EXT)
-        else:
-            src, dst = slice(ROWS, RADIUS + ROWS), slice(0, RADIUS)
-        return pltpu.make_async_remote_copy(
-            src_ref=held.at[4:6, src],
-            dst_ref=held.at[4 - 2 * k : 6 - 2 * k, dst],
-            send_sem=rim_send.at[i], recv_sem=rim_recv.at[i],
-            device_id=at(k, dt), device_id_type=MESH,
-        )
-
-    near = [sec_copy(-1, 0), sec_copy(1, 1)]
-    near += [rim_copy(k, dt, 2 * i + (dt > 0)) for i, k in enumerate((0, -1, 1)) for dt in (-1, 1)]
-    far = [sec_copy(-2, 2), sec_copy(2, 3)]
-    far += [rim_copy(k, dt, 6 + 2 * i + (dt > 0)) for i, k in enumerate((-2, 2)) for dt in (-1, 1)]
-    for copy in near + far:
-        copy.start()
+                write(y + h, d[:, h * COLS : (h + 1) * COLS])
+
+    def near_copies(s):
+        copies = []
+        for i, k in enumerate((0, -1, 1)):
+            for dt in (-1, 0, 1):
+                if (k, dt) == (0, 0):
+                    continue
+                src, dst = {
+                    -1: (slice(RADIUS, 2 * RADIUS), slice(RADIUS + ROWS, EXT)),
+                    0: (slice(RADIUS, RADIUS + ROWS), slice(RADIUS, RADIUS + ROWS)),
+                    1: (slice(ROWS, RADIUS + ROWS), slice(0, RADIUS)),
+                }[dt]
+                copies.append(pltpu.make_async_remote_copy(
+                    src_ref=held.at[2 + s, src], dst_ref=held.at[2 + s - 2 * k, dst],
+                    send_sem=near_send.at[s, 3 * i + dt + 1], recv_sem=near_recv.at[s, 3 * i + dt + 1],
+                    device_id=at(k, dt), device_id_type=MESH,
+                ))
+        return copies
+
+    def encode_own(s, carry):
+        def write(y, d):
+            held[2 + s, RADIUS + y] = d
+            desc_cy[s, pl.ds(y, DESC, stride=ROWS), :] = d.astype(F32)
+
+        encode(own_img[s, 0:16], img[s], own_img[s, 48:64], link(base + s, 0), link(base + s, 1), 0, write)
+        for copy in near_copies(s):
+            copy.start()
+        return carry
+
+    lax.fori_loop(0, 2, encode_own, 0)
+
+    def partner_links(s, j):
+        ahead, behind = base + s + OFFSETS[j], base + s - OFFSETS[j]
+        flag = partners[s, j] == ahead
+        return flag, jnp.where(flag, link(ahead, 0), link(behind, 0)), jnp.where(flag, link(ahead, 1), link(behind, 1))
+
+    for copy in img_copies[2:]:
+        copy.wait_recv()
+
+    def encode_far(s, carry):
+        flag, lower, upper = partner_links(s, 2)
+
+        def write(y, d):
+            d = d.astype(F32)
+            if y < 0:
+                d = d * lower
+            elif y >= ROWS:
+                d = d * upper
+            far_part[s, pl.ds(y + RADIUS, DESC, stride=EXT), :] = d
+
+        chosen = jnp.where(flag, far_img[1, s].astype(F32), far_img[0, s].astype(F32)).astype(BF16)
+        encode(chosen[0:16], chosen[16:48], chosen[48:64], lower, upper, RADIUS, write)
+        return carry
+
+    lax.fori_loop(0, 2, encode_far, 0)
 
     lane = lax.broadcasted_iota(jnp.int32, (COLS, COLS), 1)
 
@@ -208,22 +229,20 @@
             device_id=at(0, 2 * direction - 1), device_id_type=MESH,
         )
 
-    def correlate(j, s):
-        n = 2 * j + s
-        offset = OFFSETS[j]
-        own_id = base + s
-        flag = partners[s, j] == own_id + offset
-        lower = jnp.where(flag, link(own_id + offset, 0), link(own_id - offset, 0))
-        upper = jnp.where(flag, link(own_id + offset, 1), link(own_id - offset, 1))
-
-        def gather(y, carry):
-            ahead = held[4 + s + offset, y].astype(F32)
-            behind = held[4 + s - offset, y].astype(F32)
+    def gather(j, s):
+        flag, lower, upper = partner_links(s, j)
+
+        def row(y, carry):
+            ahead = held[2 + s + OFFSETS[j], y].astype(F32)
+            behind = held[2 + s - OFFSETS[j], y].astype(F32)
             m = jnp.where(y < RADIUS, lower, jnp.where(y >= RADIUS + ROWS, upper, 1.0))
             part[pl.ds(y, DESC, stride=EXT), :] = jnp.where(flag, ahead, behind) * m
             return carry
 
-        lax.fori_loop(0, EXT, gather, 0)
+        lax.fori_loop(0, EXT, row, 0, unroll=4)
+
+    def correlate(j, s, part):
+        n = 2 * j + s
 
         def column(b, carry):
             def channel(c, acc):
@@ -248,19 +267,27 @@
         for direction in (0, 1):
             edge_copy(0, n, direction).start()
 
-    for j in range(3):
-        if j == 0:
-            for copy in near:
-                copy.wait_recv()
-        if j == 2:
-            for copy in far:
-                copy.wait_recv()
-
-        def one(s, carry, j=j):
-            correlate(j, s)
-            return carry
-
-        lax.fori_loop(0, 2, one, 0)
+    def far_slot(s, carry):
+        correlate(2, s, far_part.at[s])
+        return carry
+
+    lax.fori_loop(0, 2, far_slot, 0)
+
+    def near_wait(s, carry):
+        for copy in near_copies(s):
+            copy.wait_recv()
+        return carry
+
+    lax.fori_loop(0, 2, near_wait, 0)
+
+    for j in range(2):
+
+        def near_slot(s, carry, j=j):
+            gather(j, s)
+            correlate(j, s, part)
+            return carry
+
+        lax.fori_loop(0, 2, near_slot, 0)
 
     def hidden_rows(n, q, o, buf):
         for h in range(2):
@@ -268,7 +295,8 @@
             for ky in range(3):
                 buf[n, 2 * q + h + 2 - ky, ky * CH : (ky + 1) * CH, :] = v
 
-    def decode_one(n, carry):
+    def decode_one(i, carry):
+        n = lax.rem(i + 4, 6)
         s = lax.rem(n, 2)
         for direction in (0, 1):
             edge_copy(0, n, direction).wait_recv()
@@ -281,7 +309,7 @@
             hidden_rows(n, q, dot(d1m[...], x.astype(BF16)), hid1)
             return carry
 
-        lax.fori_loop(0, ROWS // 2, rows, 0)
+        lax.fori_loop(0, ROWS // 2, rows, 0, unroll=8)
         for direction in (0, 1):
             edge_copy(1, n, direction).start()
         return carry
@@ -296,7 +324,8 @@
         top = slice(2 * CH, 3 * CH)
         buf[n, ROWS, top, :] = (buf[n, ROWS, top, :].astype(F32) * link(base + s, 1)).astype(BF16)
 
-    def decode_two(n, carry):
+    def decode_two(i, carry):
+        n = lax.rem(i + 4, 6)
         rims(1, n, hid1)
 
         def rows(q, carry):
@@ -304,14 +333,15 @@
             hidden_rows(n, q, dot(d2m[...], x), hid2)
             return carry
 
-        lax.fori_loop(0, ROWS // 2, rows, 0)
+        lax.fori_loop(0, ROWS // 2, rows, 0, unroll=8)
         for direction in (0, 1):
             edge_copy(2, n, direction).start()
         return carry
 
     lax.fori_loop(0, 6, decode_two, 0)
 
-    def decode_three(n, carry):
+    def decode_three(i, carry):
+        n = lax.rem(i + 4, 6)
         rims(2, n, hid2)
         weights = d3m[...].astype(BF16)
 
@@ -322,7 +352,7 @@
                 flow_y[pl.ds(pl.multiple_of((2 * q + h) * 8, 8), 8), :] = fold(o, h, 1, 8)
             return carry
 
-        lax.fori_loop(0, ROWS // 2, rows, 0)
+        lax.fori_loop(0, ROWS // 2, rows, 0, unroll=8)
         s, j = lax.rem(n, 2), n // 2
         for o in range(2):
             flow_out[s, j, o] = flow_y[pl.ds(o, ROWS, stride=8), :]
@@ -330,10 +360,15 @@
 
     lax.fori_loop(0, 6, decode_three, 0)
 
-    for direction in (0, 1):
-        pass
-    for copy in near + far:
+    for copy in img_copies:
         copy.wait_send()
+
+    def near_drain(s, carry):
+        for copy in near_copies(s):
+            copy.wait_send()
+        return carry
+
+    lax.fori_loop(0, 2, near_drain, 0)
 
     def drain(n, carry):
         for stage in range(3):
@@ -361,8 +396,8 @@
             in_specs=[smem, smem] + [vmem] * 7,
             out_specs=(vmem, vmem),
             scratch_shapes=[
-                pltpu.VMEM((2, 16, 256), BF16),
-                pltpu.VMEM((2, 16, 256), BF16),
+                pltpu.VMEM((2, 64, 256), BF16),
+                pltpu.VMEM((2, 2, 64, 256), BF16),
                 pltpu.VMEM((192, COLS), F32),
                 pltpu.VMEM((256, 3 * COLS), BF16),
                 pltpu.VMEM((CH, 16), BF16),
@@ -371,18 +406,19 @@
                 pltpu.VMEM((3 * CH, K1), BF16),
                 pltpu.VMEM((3 * CH, 3 * CH), BF16),
                 pltpu.VMEM((24, 3 * CH), F32),
-                pltpu.VMEM((24, 3 * CH, COLS), BF16),
+                pltpu.VMEM((EXT, 3 * CH, COLS), BF16),
                 pltpu.VMEM((2, DESC * ROWS, COLS), F32),
                 pltpu.VMEM((2, SPAN, DESC * ROWS, COLS), F32),
-                pltpu.VMEM((10, EXT, DESC, COLS), BF16),
+                pltpu.VMEM((6, EXT, DESC, COLS), BF16),
                 pltpu.VMEM((DESC * EXT, COLS), F32),
+                pltpu.VMEM((2, DESC * EXT, COLS), F32),
                 pltpu.VMEM((6, (ROWS + 2) * K1, COLS), F32),
                 pltpu.VMEM((6, 2, 88, COLS), F32),
                 pltpu.VMEM((6, 2, 88, COLS), F32),
                 pltpu.VMEM((6, ROWS + 2, 3 * CH, COLS), BF16),
                 pltpu.VMEM((6, ROWS + 2, 3 * CH, COLS), BF16),
                 pltpu.VMEM((ROWS * 8, COLS), F32),
-                dma((2,)), dma((2,)), dma((4,)), dma((4,)), dma((10,)), dma((10,)),
+                dma((8,)), dma((8,)), dma((2, 9)), dma((2, 9)),
                 dma((3, 6, 2)), dma((3, 6, 2)),
             ],
             compiler_params=pltpu.CompilerParams(

time: 101 us -> 58.8 us (0.58)
  Pallas kernels: 97.1 us -> 55.7 us
    pallas_call x1, Pallas kernels: 97.1 us -> 55.7 us  [shards(): pl.pallas_call(functools.partial(kernel, n_sec, n_tile), out_shape=(jax.S...]
where the time goes in v1:
time: 58.8 us; the launch traced here: 58.7 us
  Pallas kernels  55.7 us (95%)
  local copies, waits for them, and re-layouts  2.35 us (4%)
  between operations  0.65 us (1%)
    pallas_call x1, Pallas kernels, shards(): pl.pallas_call(functools.partial(kernel, n_sec, n_tile), out_shape=(jax.S...  55.7 us
    unnamed x4, local copies, waits for them, and re-layouts  2.35 us

profile of v1, /device:TPU:1, one launch (start us, length us, event | category | flops | bytes accessed | tf_op | source)
XLA Modules:
  0.0 58.7 jit_solution(1592092857058497353)
XLA Ops:
  0.6 55.7 %shard_map.104 = (bf16[2,32,16,128]{3,2,1,0:T(8,128)(2,1)}, f32[2,3,2,16,128]{4,3,2,1,0:T(8,128)}) custom-call(s32[3,64]{1,0:T(4,128)} %bitcast.15, s32[2,3]{1,0:T(2,128)} %partners.1, bf16[2,32,256]{2,1,0:T(8,128)(2,1)} %img.1, bf16[3,3,64]{2,1,0:T(4,128)(2,1)} %bitcast.14, bf16[3,3,64,64]{3,2,1,0:T(8,128)(2,1)} %bitcast.9, bf16[32,64]{1,0:T(8,128)(2,1)} %bitcast.12, ...), custom_call_target="tpu_custom_call" | custom-call | tf_op jit(solution)/shard_map/pallas_call | solution.py:390
  56.3 0.0 copy-start
  56.3 1.7 %copy.13 = bf16[2,32,16,128]{3,2,1,0:T(8,128)(2,1)} copy(bf16[2,32,16,128]{3,2,1,0:T(8,128)(2,1)} %get-tuple-element.4) | data formatting | bytes 524288
  58.0 0.0 copy-done
  58.0 0.6 %copy.14 = f32[2,3,2,16,128]{4,3,2,1,0:T(8,128)} copy(f32[2,3,2,16,128]{4,3,2,1,0:T(8,128)S(1)} %copy-done) | data formatting | bytes 196608
Async XLA Ops:
  56.3 1.7 %copy-start = (f32[2,3,2,16,128]{4,3,2,1,0:T(8,128)S(1)}, f32[2,3,2,16,128]{4,3,2,1,0:T(8,128)}, u32[]{:S(2)}) copy-start(f32[2,3,2,16,128]{4,3,2,1,0:T(8,128)} %get-tuple-element.5) | copy-start | bytes 294916

commit v2 on v1

--- a/solution.py
+++ b/solution.py
@@ -19,7 +19,9 @@
 COLS = 128
 CH = 64
 DESC = 32
-K1 = 248
+EVEN = DISP - 1
+PAD = EVEN + 8
+K1 = 3 * EVEN + 8
 EXT = ROWS + 2 * RADIUS
 
 
@@ -45,8 +47,8 @@
 
 def kernel(
     n_sec, n_tile, seam, partners, img, w1, w2, w3, d1, d2, d3, desc_out, flow_out,
-    own_img, far_img, taps, pick, w1m, w2m, w3m, d1m, d2m, d3m, first3, desc_cy, own_rot, held, part, far_part,
-    cost3, edge_out, edge_in, hid1, hid2, flow_y,
+    own_img, far_img, taps, pick, w1m, w2m, w3m, d1m, d2m, d3m, first3, second, desc_cy, own_rot, held, part, raw,
+    cost, hid1, hid2, flow_y,
     img_send, img_recv, near_send, near_recv, edge_send, edge_recv,
 ):
     sec, tile = lax.axis_index("sec"), lax.axis_index("tile")
@@ -96,14 +98,18 @@
         w2m[rows, :] = jnp.concatenate([w2[ky, kx].astype(F32) for ky in range(3)], axis=1).astype(BF16)
         d2m[rows, :] = jnp.concatenate([d2[ky, kx].astype(F32) for ky in range(3)], axis=1).astype(BF16)
         d1m[rows, :] = jnp.concatenate(
-            [d1[ky, kx].astype(F32) for ky in range(3)] + [jnp.zeros((CH, K1 - 3 * DISP), F32)], axis=1
+            [d1[ky, kx].astype(F32)[:, 0:EVEN] for ky in range(3)]
+            + [d1[ky, kx].astype(F32)[:, EVEN:DISP] for ky in range(3)]
+            + [jnp.zeros((CH, K1 - 3 * DISP), F32)],
+            axis=1,
         ).astype(BF16)
     d3m[...] = jnp.zeros_like(d3m)
     for kx in range(3):
         d3m[kx * 8 : kx * 8 + 2, :] = jnp.concatenate([d3[ky, kx].astype(F32) for ky in range(3)], axis=1)
+    raw[...] = jnp.zeros_like(raw)
     for n in range(6):
-        for y in range(ROWS + 2):
-            cost3[n, y * K1 + 240 : y * K1 + K1, :] = jnp.zeros((8, COLS), F32)
+        for y in [*range(1, ROWS + 1), *range(ROWS + 2, ROWS + 7)]:
+            cost[n, y * PAD + EVEN : (y + 1) * PAD, :] = jnp.zeros((8, COLS), F32)
 
     for copy in img_copies[:2]:
         copy.wait_recv()
@@ -137,28 +143,34 @@
         for y in range(-rim, ROWS + rim, 2):
             x = jnp.concatenate([first3[y + RADIUS], first3[y + RADIUS + 1]], axis=1)
             o = dot(w2m[...], x)
-            z = jnp.concatenate([leaky(fold(o, h, 2, CH)).astype(BF16) for h in range(2)], axis=1)
+            for h in range(2):
+                second[y + h + RADIUS] = leaky(fold(o, h, 2, CH)).astype(BF16)
+
+        for y in range(-rim, ROWS + rim, 2):
+            z = jnp.concatenate([second[y + RADIUS], second[y + RADIUS + 1]], axis=1)
             d = dot(w3m[...], z).astype(BF16)
             for h in range(2):
                 write(y + h, d[:, h * COLS : (h + 1) * COLS])
 
-    def near_copies(s):
-        copies = []
-        for i, k in enumerate((0, -1, 1)):
-            for dt in (-1, 0, 1):
-                if (k, dt) == (0, 0):
-                    continue
-                src, dst = {
-                    -1: (slice(RADIUS, 2 * RADIUS), slice(RADIUS + ROWS, EXT)),
-                    0: (slice(RADIUS, RADIUS + ROWS), slice(RADIUS, RADIUS + ROWS)),
-                    1: (slice(ROWS, RADIUS + ROWS), slice(0, RADIUS)),
-                }[dt]
-                copies.append(pltpu.make_async_remote_copy(
-                    src_ref=held.at[2 + s, src], dst_ref=held.at[2 + s - 2 * k, dst],
-                    send_sem=near_send.at[s, 3 * i + dt + 1], recv_sem=near_recv.at[s, 3 * i + dt + 1],
-                    device_id=at(k, dt), device_id_type=MESH,
-                ))
-        return copies
+    RIMS = {
+        -1: (slice(RADIUS, 2 * RADIUS), slice(RADIUS + ROWS, EXT)),
+        0: (slice(RADIUS, RADIUS + ROWS), slice(RADIUS, RADIUS + ROWS)),
+        1: (slice(ROWS, RADIUS + ROWS), slice(0, RADIUS)),
+    }
+
+    def near_copy(s, k, dt, i):
+        src, dst = RIMS[dt]
+        return pltpu.make_async_remote_copy(
+            src_ref=held.at[2 + s, src], dst_ref=held.at[2 + s - 2 * k, dst],
+            send_sem=near_send.at[s, i], recv_sem=near_recv.at[s, i],
+            device_id=at(k, dt), device_id_type=MESH,
+        )
+
+    def near_copies(s, batch):
+        if batch == 0:
+            k = 2 * s - 1
+            return [near_copy(s, k, dt, dt + 1) for dt in (0, -1, 1)] + [near_copy(s, 0, -1, 3), near_copy(s, 0, 1, 4)]
+        return [near_copy(s, 1 - 2 * s, dt, dt + 6) for dt in (0, -1, 1)]
 
     def encode_own(s, carry):
         def write(y, d):
@@ -166,11 +178,18 @@
             desc_cy[s, pl.ds(y, DESC, stride=ROWS), :] = d.astype(F32)
 
         encode(own_img[s, 0:16], img[s], own_img[s, 48:64], link(base + s, 0), link(base + s, 1), 0, write)
-        for copy in near_copies(s):
+        for copy in near_copies(s, 0):
             copy.start()
         return carry
 
     lax.fori_loop(0, 2, encode_own, 0)
+
+    def near_rest(s, carry):
+        for copy in near_copies(s, 1):
+            copy.start()
+        return carry
+
+    lax.fori_loop(0, 2, near_rest, 0)
 
     def partner_links(s, j):
         ahead, behind = base + s + OFFSETS[j], base + s - OFFSETS[j]
@@ -189,7 +208,7 @@
                 d = d * lower
             elif y >= ROWS:
                 d = d * upper
-            far_part[s, pl.ds(y + RADIUS, DESC, stride=EXT), :] = d
+            part[4 + s, pl.ds(y + RADIUS, DESC, stride=EXT), :] = d
 
         chosen = jnp.where(flag, far_img[1, s].astype(F32), far_img[0, s].astype(F32)).astype(BF16)
         encode(chosen[0:16], chosen[16:48], chosen[48:64], lower, upper, RADIUS, write)
@@ -216,7 +235,9 @@
 
     def edge_copy(stage, n, direction):
         if stage == 0:
-            src, dst = edge_out.at[n, direction], edge_in.at[n, direction]
+            at_src, at_dst = ((1, ROWS + 1), (ROWS, 0))[direction]
+            src = cost.at[n, at_src * PAD : (at_src + 1) * PAD]
+            dst = cost.at[n, at_dst * PAD : (at_dst + 1) * PAD]
         else:
             buf = (hid1, hid2)[stage - 1]
             if direction == 0:
@@ -236,58 +257,45 @@
             ahead = held[2 + s + OFFSETS[j], y].astype(F32)
             behind = held[2 + s - OFFSETS[j], y].astype(F32)
             m = jnp.where(y < RADIUS, lower, jnp.where(y >= RADIUS + ROWS, upper, 1.0))
-            part[pl.ds(y, DESC, stride=EXT), :] = jnp.where(flag, ahead, behind) * m
+            part[2 * j + s, pl.ds(y, DESC, stride=EXT), :] = jnp.where(flag, ahead, behind) * m
             return carry
 
         lax.fori_loop(0, EXT, row, 0, unroll=4)
 
-    def correlate(j, s, part):
-        n = 2 * j + s
+    def near_parts(j):
+        for s in range(2):
+            for copy in near_copies(s, j):
+                copy.wait_recv()
+        lax.fori_loop(0, 2, lambda s, carry: (gather(j, s), carry)[1], 0)
+
+    def correlate(i, carry):
+        n = lax.rem(i + 4, 6)
+        s = lax.rem(n, 2)
+        pl.when(i == 2)(lambda: near_parts(0))
+        pl.when(i == 4)(lambda: near_parts(1))
+
+        def place(b):
+            for a in range(SPAN):
+                moved = pltpu.roll(raw[a], lax.rem(COLS + RADIUS - b, COLS), 1)
+                cost[n, pl.ds(PAD + a * SPAN + b, ROWS, stride=PAD), :] = moved
 
         def column(b, carry):
-            def channel(c, acc):
-                own = own_rot[s, b, pl.ds(pl.multiple_of(c * ROWS, ROWS), ROWS), :]
-                start = pl.multiple_of(c * EXT, 8)
-                return tuple(acc[a] + own * part[pl.ds(start + a, ROWS), :] for a in range(SPAN))
-
-            acc = lax.fori_loop(
-                0, DESC, channel, tuple(jnp.zeros((ROWS, COLS), F32) for _ in range(SPAN)), unroll=4
-            )
-            shift = lax.rem(COLS + RADIUS - b, COLS)
+            place(jnp.maximum(b - 1, 0))
+            acc = [None] * SPAN
+            for c in range(DESC):
+                own = own_rot[s, b, c * ROWS : (c + 1) * ROWS, :]
+                for a in range(SPAN):
+                    term = own * part[n, c * EXT + a : c * EXT + a + ROWS, :]
+                    acc[a] = term if c == 0 else acc[a] + term
             for a in range(SPAN):
-                moved = pltpu.roll(acc[a], shift, 1)
-                d = a * SPAN + b
-                for ky in range(3):
-                    cost3[n, pl.ds((2 - ky) * K1 + ky * DISP + d, ROWS, stride=K1), :] = moved
+                raw[a] = acc[a]
             return carry
 
         lax.fori_loop(0, SPAN, column, 0)
-        edge_out[n, 0] = cost3[n, K1 + DISP : K1 + DISP + 88, :]
-        edge_out[n, 1] = cost3[n, ROWS * K1 + DISP : ROWS * K1 + DISP + 88, :]
+        place(SPAN - 1)
         for direction in (0, 1):
             edge_copy(0, n, direction).start()
-
-    def far_slot(s, carry):
-        correlate(2, s, far_part.at[s])
-        return carry
-
-    lax.fori_loop(0, 2, far_slot, 0)
-
-    def near_wait(s, carry):
-        for copy in near_copies(s):
-            copy.wait_recv()
-        return carry
-
-    lax.fori_loop(0, 2, near_wait, 0)
-
-    for j in range(2):
-
-        def near_slot(s, carry, j=j):
-            gather(j, s)
-            correlate(j, s, part)
-            return carry
-
-        lax.fori_loop(0, 2, near_slot, 0)
+        return carry
 
     def hidden_rows(n, q, o, buf):
         for h in range(2):
@@ -300,12 +308,20 @@
         s = lax.rem(n, 2)
         for direction in (0, 1):
             edge_copy(0, n, direction).wait_recv()
-        cost3[n, K1 : K1 + DISP, :] = edge_in[n, 1, 0:DISP, :] * link(base + s, 0)
-        cost3[n, ROWS * K1 + 2 * DISP : ROWS * K1 + 3 * DISP, :] = edge_in[n, 0, 0:DISP, :] * link(base + s, 1)
+        cost[n, 0:PAD, :] = cost[n, 0:PAD, :] * link(base + s, 0)
+        top = slice((ROWS + 1) * PAD, (ROWS + 2) * PAD)
+        cost[n, top, :] = cost[n, top, :] * link(base + s, 1)
 
         def rows(q, carry):
-            start = pl.multiple_of((2 * q + 1) * K1, 8)
-            x = jnp.concatenate([cost3[n, pl.ds(start, K1), :], cost3[n, pl.ds(start + K1, K1), :]], axis=1)
+            taps_of = []
+            for h in range(2):
+                start = pl.multiple_of((2 * q + h) * PAD, 8)
+                taps_of.append(jnp.concatenate(
+                    [cost[n, pl.ds(start + ky * PAD, EVEN), :] for ky in range(3)]
+                    + [cost[n, pl.ds(start + EVEN, 8, stride=PAD), :]],
+                    axis=0,
+                ))
+            x = jnp.concatenate(taps_of, axis=1)
             hidden_rows(n, q, dot(d1m[...], x.astype(BF16)), hid1)
             return carry
 
@@ -314,7 +330,6 @@
             edge_copy(1, n, direction).start()
         return carry
 
-    lax.fori_loop(0, 6, decode_one, 0)
 
     def rims(stage, n, buf):
         s = lax.rem(n, 2)
@@ -338,7 +353,6 @@
             edge_copy(2, n, direction).start()
         return carry
 
-    lax.fori_loop(0, 6, decode_two, 0)
 
     def decode_three(i, carry):
         n = lax.rem(i + 4, 6)
@@ -358,13 +372,17 @@
             flow_out[s, j, o] = flow_y[pl.ds(o, ROWS, stride=8), :]
         return carry
 
+
+    lax.fori_loop(0, 6, correlate, 0)
+    lax.fori_loop(0, 6, decode_one, 0)
+    lax.fori_loop(0, 6, decode_two, 0)
     lax.fori_loop(0, 6, decode_three, 0)
 
     for copy in img_copies:
         copy.wait_send()
 
     def near_drain(s, carry):
-        for copy in near_copies(s):
+        for copy in near_copies(s, 0) + near_copies(s, 1):
             copy.wait_send()
         return carry
 
@@ -407,14 +425,13 @@
                 pltpu.VMEM((3 * CH, 3 * CH), BF16),
                 pltpu.VMEM((24, 3 * CH), F32),
                 pltpu.VMEM((EXT, 3 * CH, COLS), BF16),
+                pltpu.VMEM((EXT, CH, COLS), BF16),
                 pltpu.VMEM((2, DESC * ROWS, COLS), F32),
                 pltpu.VMEM((2, SPAN, DESC * ROWS, COLS), F32),
                 pltpu.VMEM((6, EXT, DESC, COLS), BF16),
-                pltpu.VMEM((DESC * EXT, COLS), F32),
-                pltpu.VMEM((2, DESC * EXT, COLS), F32),
-                pltpu.VMEM((6, (ROWS + 2) * K1, COLS), F32),
-                pltpu.VMEM((6, 2, 88, COLS), F32),
-                pltpu.VMEM((6, 2, 88, COLS), F32),
+                pltpu.VMEM((6, DESC * EXT, COLS), F32),
+                pltpu.VMEM((SPAN, ROWS, COLS), F32),
+                pltpu.VMEM((6, (ROWS + 7) * PAD, COLS), F32),
                 pltpu.VMEM((6, ROWS + 2, 3 * CH, COLS), BF16),
                 pltpu.VMEM((6, ROWS + 2, 3 * CH, COLS), BF16),
                 pltpu.VMEM((ROWS * 8, COLS), F32),

time: 58.8 us -> 46.2 us (0.79)
  Pallas kernels: 55.7 us -> 43.1 us
    pallas_call x1, Pallas kernels: 55.7 us -> 43.1 us  [shards(): pl.pallas_call(functools.partial(kernel, n_sec, n_tile), out_shape=(jax.S...]
where the time goes in v2:
time: 46.2 us; the launch traced here: 46.1 us
  Pallas kernels  43.1 us (93%)
  local copies, waits for them, and re-layouts  2.35 us (5%)
  between operations  0.65 us (1%)
    pallas_call x1, Pallas kernels, shards(): pl.pallas_call(functools.partial(kernel, n_sec, n_tile), out_shape=(jax.S...  43.1 us
    unnamed x4, local copies, waits for them, and re-layouts  2.35 us

profile of v2, /device:TPU:1, one launch (start us, length us, event | category | flops | bytes accessed | tf_op | source)
XLA Modules:
  0.0 46.1 jit_solution(11294932793133934432)
XLA Ops:
  0.6 43.1 %shard_map.104 = (bf16[2,32,16,128]{3,2,1,0:T(8,128)(2,1)}, f32[2,3,2,16,128]{4,3,2,1,0:T(8,128)}) custom-call(s32[3,64]{1,0:T(4,128)} %bitcast.15, s32[2,3]{1,0:T(2,128)} %partners.1, bf16[2,32,256]{2,1,0:T(8,128)(2,1)} %img.1, bf16[3,3,64]{2,1,0:T(4,128)(2,1)} %bitcast.14, bf16[3,3,64,64]{3,2,1,0:T(8,128)(2,1)} %bitcast.9, bf16[32,64]{1,0:T(8,128)(2,1)} %bitcast.12, ...), custom_call_target="tpu_custom_call" | custom-call | tf_op jit(solution)/shard_map/pallas_call | solution.py:408
  43.7 0.0 copy-start
  43.7 1.7 %copy.13 = bf16[2,32,16,128]{3,2,1,0:T(8,128)(2,1)} copy(bf16[2,32,16,128]{3,2,1,0:T(8,128)(2,1)} %get-tuple-element.4) | data formatting | bytes 524288
  45.4 0.0 copy-done
  45.5 0.6 %copy.14 = f32[2,3,2,16,128]{4,3,2,1,0:T(8,128)} copy(f32[2,3,2,16,128]{4,3,2,1,0:T(8,128)S(1)} %copy-done) | data formatting | bytes 196608
Async XLA Ops:
  43.7 1.7 %copy-start = (f32[2,3,2,16,128]{4,3,2,1,0:T(8,128)S(1)}, f32[2,3,2,16,128]{4,3,2,1,0:T(8,128)}, u32[]{:S(2)}) copy-start(f32[2,3,2,16,128]{4,3,2,1,0:T(8,128)} %get-tuple-element.5) | copy-start | bytes 294916

commit v3 on v2

--- a/solution.py
+++ b/solution.py
@@ -77,20 +77,6 @@
         place = jnp.clip(place, 0, n_tile - 2)
         section = jnp.clip(section, 0, 2 * n_sec - 1)
         return jnp.where(inside, seam[place, section], 0).astype(F32)
-
-    pl.semaphore_wait(barrier, len(peers))
-
-    def img_copy(k, dt, i):
-        dst = own_img if k == 0 else far_img.at[int(k < 0)]
-        src, rows = {-1: (img.at[:, 0:16], slice(48, 64)), 0: (img, slice(16, 48)), 1: (img.at[:, 16:32], slice(0, 16))}[dt]
-        return pltpu.make_async_remote_copy(
-            src_ref=src, dst_ref=dst.at[:, rows], send_sem=img_send.at[i], recv_sem=img_recv.at[i],
-            device_id=at(k, dt), device_id_type=MESH,
-        )
-
-    img_copies = [img_copy(k, dt, i) for i, (k, dt) in enumerate([p for p in peers if p[0] in (0, -2, 2)])]
-    for copy in img_copies:
-        copy.start()
 
     w3m[...] = w3[...]
     for kx in range(3):
@@ -111,6 +97,20 @@
         for y in [*range(1, ROWS + 1), *range(ROWS + 2, ROWS + 7)]:
             cost[n, y * PAD + EVEN : (y + 1) * PAD, :] = jnp.zeros((8, COLS), F32)
 
+    pl.semaphore_wait(barrier, len(peers))
+
+    def img_copy(k, dt, i):
+        dst = own_img if k == 0 else far_img.at[int(k < 0)]
+        src, rows = {-1: (img.at[:, 0:16], slice(48, 64)), 0: (img, slice(16, 48)), 1: (img.at[:, 16:32], slice(0, 16))}[dt]
+        return pltpu.make_async_remote_copy(
+            src_ref=src, dst_ref=dst.at[:, rows], send_sem=img_send.at[i], recv_sem=img_recv.at[i],
+            device_id=at(k, dt), device_id_type=MESH,
+        )
+
+    img_copies = [img_copy(k, dt, i) for i, (k, dt) in enumerate([p for p in peers if p[0] in (0, -2, 2)])]
+    for copy in img_copies:
+        copy.start()
+
     for copy in img_copies[:2]:
         copy.wait_recv()
 
@@ -196,26 +196,6 @@
         flag = partners[s, j] == ahead
         return flag, jnp.where(flag, link(ahead, 0), link(behind, 0)), jnp.where(flag, link(ahead, 1), link(behind, 1))
 
-    for copy in img_copies[2:]:
-        copy.wait_recv()
-
-    def encode_far(s, carry):
-        flag, lower, upper = partner_links(s, 2)
-
-        def write(y, d):
-            d = d.astype(F32)
-            if y < 0:
-                d = d * lower
-            elif y >= ROWS:
-                d = d * upper
-            part[4 + s, pl.ds(y + RADIUS, DESC, stride=EXT), :] = d
-
-        chosen = jnp.where(flag, far_img[1, s].astype(F32), far_img[0, s].astype(F32)).astype(BF16)
-        encode(chosen[0:16], chosen[16:48], chosen[48:64], lower, upper, RADIUS, write)
-        return carry
-
-    lax.fori_loop(0, 2, encode_far, 0)
-
     lane = lax.broadcasted_iota(jnp.int32, (COLS, COLS), 1)
 
     def spread(i, carry):
@@ -232,6 +212,26 @@
         return carry
 
     lax.fori_loop(0, 8, spread, 0)
+
+    for copy in img_copies[2:]:
+        copy.wait_recv()
+
+    def encode_far(s, carry):
+        flag, lower, upper = partner_links(s, 2)
+
+        def write(y, d):
+            d = d.astype(F32)
+            if y < 0:
+                d = d * lower
+            elif y >= ROWS:
+                d = d * upper
+            part[4 + s, pl.ds(y + RADIUS, DESC, stride=EXT), :] = d
+
+        chosen = jnp.where(flag, far_img[1, s].astype(F32), far_img[0, s].astype(F32)).astype(BF16)
+        encode(chosen[0:16], chosen[16:48], chosen[48:64], lower, upper, RADIUS, write)
+        return carry
+
+    lax.fori_loop(0, 2, encode_far, 0)
 
     def edge_copy(stage, n, direction):
         if stage == 0:

time: 46.2 us -> 45.9 us (level)
  no operation moved by 1% of the time
where the time goes in v3:
time: 45.9 us; the launch traced here: 45.7 us
  Pallas kernels  42.7 us (93%)
  local copies, waits for them, and re-layouts  2.35 us (5%)
  between operations  0.65 us (1%)
    pallas_call x1, Pallas kernels, shards(): pl.pallas_call(functools.partial(kernel, n_sec, n_tile), out_shape=(jax.S...  42.7 us
    unnamed x4, local copies, waits for them, and re-layouts  2.35 us

profile of v3, /device:TPU:1, one launch (start us, length us, event | category | flops | bytes accessed | tf_op | source)
XLA Modules:
  0.0 45.7 jit_solution(4902973402549577156)
XLA Ops:
  0.6 42.7 %shard_map.104 = (bf16[2,32,16,128]{3,2,1,0:T(8,128)(2,1)}, f32[2,3,2,16,128]{4,3,2,1,0:T(8,128)}) custom-call(s32[3,64]{1,0:T(4,128)} %bitcast.15, s32[2,3]{1,0:T(2,128)} %partners.1, bf16[2,32,256]{2,1,0:T(8,128)(2,1)} %img.1, bf16[3,3,64]{2,1,0:T(4,128)(2,1)} %bitcast.14, bf16[3,3,64,64]{3,2,1,0:T(8,128)(2,1)} %bitcast.9, bf16[32,64]{1,0:T(8,128)(2,1)} %bitcast.12, ...), custom_call_target="tpu_custom_call" | custom-call | tf_op jit(solution)/shard_map/pallas_call | solution.py:408
  43.3 0.0 copy-start
  43.4 1.7 %copy.13 = bf16[2,32,16,128]{3,2,1,0:T(8,128)(2,1)} copy(bf16[2,32,16,128]{3,2,1,0:T(8,128)(2,1)} %get-tuple-element.4) | data formatting | bytes 524288
  45.1 0.0 copy-done
  45.1 0.6 %copy.14 = f32[2,3,2,16,128]{4,3,2,1,0:T(8,128)} copy(f32[2,3,2,16,128]{4,3,2,1,0:T(8,128)S(1)} %copy-done) | data formatting | bytes 196608
Async XLA Ops:
  43.3 1.7 %copy-start = (f32[2,3,2,16,128]{4,3,2,1,0:T(8,128)S(1)}, f32[2,3,2,16,128]{4,3,2,1,0:T(8,128)}, u32[]{:S(2)}) copy-start(f32[2,3,2,16,128]{4,3,2,1,0:T(8,128)} %get-tuple-element.5) | copy-start | bytes 294916

commit v4 on v3

--- a/solution.py
+++ b/solution.py
@@ -291,7 +291,7 @@
                 raw[a] = acc[a]
             return carry
 
-        lax.fori_loop(0, SPAN, column, 0)
+        lax.fori_loop(0, SPAN, column, 0, unroll=3)
         place(SPAN - 1)
         for direction in (0, 1):
             edge_copy(0, n, direction).start()

time: 45.9 us -> 45.1 us (0.983)
  Pallas kernels: 42.7 us -> 42 us
    pallas_call x1, Pallas kernels: 42.7 us -> 42 us  [shards(): pl.pallas_call(functools.partial(kernel, n_sec, n_tile), out_shape=(jax.S...]
where the time goes in v4:
time: 45.1 us; the launch traced here: 45 us
  Pallas kernels  42 us (93%)
  local copies, waits for them, and re-layouts  2.35 us (5%)
  between operations  0.65 us (1%)
    pallas_call x1, Pallas kernels, shards(): pl.pallas_call(functools.partial(kernel, n_sec, n_tile), out_shape=(jax.S...  42 us
    unnamed x4, local copies, waits for them, and re-layouts  2.35 us

profile of v4, /device:TPU:1, one launch (start us, length us, event | category | flops | bytes accessed | tf_op | source)
XLA Modules:
  0.0 45.0 jit_solution(10073959650245126550)
XLA Ops:
  0.6 42.0 %shard_map.104 = (bf16[2,32,16,128]{3,2,1,0:T(8,128)(2,1)}, f32[2,3,2,16,128]{4,3,2,1,0:T(8,128)}) custom-call(s32[3,64]{1,0:T(4,128)} %bitcast.15, s32[2,3]{1,0:T(2,128)} %partners.1, bf16[2,32,256]{2,1,0:T(8,128)(2,1)} %img.1, bf16[3,3,64]{2,1,0:T(4,128)(2,1)} %bitcast.14, bf16[3,3,64,64]{3,2,1,0:T(8,128)(2,1)} %bitcast.9, bf16[32,64]{1,0:T(8,128)(2,1)} %bitcast.12, ...), custom_call_target="tpu_custom_call" | custom-call | tf_op jit(solution)/shard_map/pallas_call | solution.py:408
  42.6 0.0 copy-start
  42.6 1.7 %copy.13 = bf16[2,32,16,128]{3,2,1,0:T(8,128)(2,1)} copy(bf16[2,32,16,128]{3,2,1,0:T(8,128)(2,1)} %get-tuple-element.4) | data formatting | bytes 524288
  44.3 0.0 copy-done
  44.3 0.6 %copy.14 = f32[2,3,2,16,128]{4,3,2,1,0:T(8,128)} copy(f32[2,3,2,16,128]{4,3,2,1,0:T(8,128)S(1)} %copy-done) | data formatting | bytes 196608
Async XLA Ops:
  42.6 1.7 %copy-start = (f32[2,3,2,16,128]{4,3,2,1,0:T(8,128)S(1)}, f32[2,3,2,16,128]{4,3,2,1,0:T(8,128)}, u32[]{:S(2)}) copy-start(f32[2,3,2,16,128]{4,3,2,1,0:T(8,128)} %get-tuple-element.5) | copy-start | bytes 294916

commit v5 on v4

--- a/solution.py
+++ b/solution.py
@@ -211,7 +211,7 @@
             own_rot[s, b, rows, :] = jnp.where(keep, moved, 0.0)
         return carry
 
-    lax.fori_loop(0, 8, spread, 0)
+    lax.fori_loop(0, 8, spread, 0, unroll=2)
 
     for copy in img_copies[2:]:
         copy.wait_recv()
@@ -260,7 +260,7 @@
             part[2 * j + s, pl.ds(y, DESC, stride=EXT), :] = jnp.where(flag, ahead, behind) * m
             return carry
 
-        lax.fori_loop(0, EXT, row, 0, unroll=4)
+        lax.fori_loop(0, EXT, row, 0, unroll=12)
 
     def near_parts(j):
         for s in range(2):
@@ -291,7 +291,7 @@
                 raw[a] = acc[a]
             return carry
 
-        lax.fori_loop(0, SPAN, column, 0, unroll=3)
+        lax.fori_loop(0, SPAN, column, 0, unroll=9)
         place(SPAN - 1)
         for direction in (0, 1):
             edge_copy(0, n, direction).start()

time: 45.1 us -> 44.3 us (0.982)
  Pallas kernels: 42 us -> 41.1 us
    pallas_call x1, Pallas kernels: 42 us -> 41.1 us  [shards(): pl.pallas_call(functools.partial(kernel, n_sec, n_tile), out_shape=(jax.S...]
where the time goes in v5:
time: 44.3 us; the launch traced here: 44.1 us
  Pallas kernels  41.1 us (93%)
  local copies, waits for them, and re-layouts  2.35 us (5%)
  between operations  0.65 us (1%)
    pallas_call x1, Pallas kernels, shards(): pl.pallas_call(functools.partial(kernel, n_sec, n_tile), out_shape=(jax.S...  41.1 us
    unnamed x4, local copies, waits for them, and re-layouts  2.35 us

profile of v5, /device:TPU:1, one launch (start us, length us, event | category | flops | bytes accessed | tf_op | source)
XLA Modules:
  0.0 44.1 jit_solution(3797335416894316570)
XLA Ops:
  0.6 41.1 %shard_map.104 = (bf16[2,32,16,128]{3,2,1,0:T(8,128)(2,1)}, f32[2,3,2,16,128]{4,3,2,1,0:T(8,128)}) custom-call(s32[3,64]{1,0:T(4,128)} %bitcast.15, s32[2,3]{1,0:T(2,128)} %partners.1, bf16[2,32,256]{2,1,0:T(8,128)(2,1)} %img.1, bf16[3,3,64]{2,1,0:T(4,128)(2,1)} %bitcast.14, bf16[3,3,64,64]{3,2,1,0:T(8,128)(2,1)} %bitcast.9, bf16[32,64]{1,0:T(8,128)(2,1)} %bitcast.12, ...), custom_call_target="tpu_custom_call" | custom-call | tf_op jit(solution)/shard_map/pallas_call | solution.py:408
  41.8 0.0 copy-start
  41.8 1.7 %copy.13 = bf16[2,32,16,128]{3,2,1,0:T(8,128)(2,1)} copy(bf16[2,32,16,128]{3,2,1,0:T(8,128)(2,1)} %get-tuple-element.4) | data formatting | bytes 524288
  43.5 0.0 copy-done
  43.5 0.6 %copy.14 = f32[2,3,2,16,128]{4,3,2,1,0:T(8,128)} copy(f32[2,3,2,16,128]{4,3,2,1,0:T(8,128)S(1)} %copy-done) | data formatting | bytes 196608
Async XLA Ops:
  41.8 1.7 %copy-start = (f32[2,3,2,16,128]{4,3,2,1,0:T(8,128)S(1)}, f32[2,3,2,16,128]{4,3,2,1,0:T(8,128)}, u32[]{:S(2)}) copy-start(f32[2,3,2,16,128]{4,3,2,1,0:T(8,128)} %get-tuple-element.5) | copy-start | bytes 294916
